TPU v7x, 256 devices: a whole 4x4x8 slice. The times are simulated.
256 devices in a mesh: row: 8 (over y, core), col: 32 (over z, x).
Axes of the slice: x: 4, y: 4, z: 8, core: 2. Of those that a mesh axis runs over, the one named last changes fastest.
Arguments:
- raw_blocks: bfloat16 [2, 16384, 16384], P(None, 'row', 'col'), may hold values from -1.25 to 1.25
- occupancy: int32 [32, 16384], P('row', 'col'), may hold values 0 or 1
- exponent: int32 [32, 32], P('row', 'col'), may hold values from -2 to 2
Outputs:
- multiples: bfloat16 [2, 2, 16384, 512], P(None, None, ('row', 'col'))
All inputs are finite; a program needn't handle non-finite values. No bound on the sum of `occupancy` on one device may be relied on, other than what follows from the above.
Results may differ from a plain program's by a relative error of at most 0.02.
Values may be sent and summed in bfloat16 or wider, within the bound.
A program may use at most 64 MiB of HBM per device.

v0:
```python
import jax
import jax.numpy as jnp
from jax import lax
from jax.sharding import PartitionSpec as P


def from_root(value, axis, source):
    kept = jnp.where(lax.axis_index(axis) == source, value, 0).astype(value.dtype)
    return lax.psum(kept, axis)


def decode_block(raw_blocks, occupancy, exponent):
    tile_rows = occupancy.shape[0]
    tile_len = raw_blocks.shape[1] // tile_rows
    panel_width = raw_blocks.shape[2]
    tile_scale = jnp.exp2(exponent.astype(jnp.float32))
    col_scale = jnp.repeat(tile_scale, panel_width // tile_scale.shape[1], axis=1)
    factor = occupancy.astype(jnp.float32) * col_scale
    shaped = (
        raw_blocks.astype(jnp.float32).reshape(2, tile_rows, tile_len, panel_width)
        * factor[None, :, None, :]
    )
    return shaped.reshape(raw_blocks.shape).astype(jnp.bfloat16)


def fetch_piece(decoded, which_panel):
    col_count = lax.axis_size("col")
    col_ratio = col_count // lax.axis_size("row")
    root_col = which_panel * (col_count // 2)
    my_col = lax.axis_index("col")
    panel_width = decoded.shape[2]
    root_block = from_root(decoded, "col", root_col)
    slab_piece = lax.dynamic_slice_in_dim(
        root_block, my_col % col_ratio * panel_width, panel_width, 1
    )
    return from_root(slab_piece, "row", my_col // col_ratio)


def complex_term(decoded, slab_piece):
    real_part = jnp.dot(decoded[0], slab_piece[0], preferred_element_type=jnp.float32) - jnp.dot(
        decoded[1], slab_piece[1], preferred_element_type=jnp.float32
    )
    imag_part = jnp.dot(decoded[0], slab_piece[1], preferred_element_type=jnp.float32) + jnp.dot(
        decoded[1], slab_piece[0], preferred_element_type=jnp.float32
    )
    return jnp.concatenate([real_part, imag_part], axis=1)


def on_device(raw_blocks, occupancy, exponent):
    decoded = decode_block(raw_blocks, occupancy, exponent)
    row_total = decoded.shape[1]
    kept_rows = row_total // lax.axis_size("col")
    panel_width = decoded.shape[2]
    results = []
    for which_panel in range(2):
        slab_piece = fetch_piece(decoded, which_panel)

        def one_term(offset, amount, slab_piece=slab_piece):
            return complex_term(decoded, slab_piece)

        results.append(
            lax.psum_scatter(
                one_term(jnp.int32(0), kept_rows * lax.axis_size("col")).astype(jnp.bfloat16),
                "col",
                scatter_dimension=0,
                tiled=True,
            ).astype(jnp.float32)
        )
    stacked = [
        jnp.transpose(result.reshape(result.shape[0], 2, panel_width), (1, 0, 2))
        for result in results
    ]
    return jnp.stack(stacked).astype(jnp.bfloat16)


def solution(mesh):
    placed = (P(None, "row", "col"), P("row", "col"), P("row", "col"))
    return jax.shard_map(
        on_device,
        mesh=mesh,
        in_specs=placed,
        out_specs=P(None, None, ("row", "col"), None),
        check_vma=False,
    )
```

profile of v0, /device:TPU:8, one launch (start us, length us, event | category | flops | bytes accessed | tf_op | source)
XLA Modules:
  0.0 772.7 jit_solution(4626452291343266356)
XLA Ops:
  7.3 0.9 convert_multiply_fusion
  8.8 2.8 broadcast_select_fusion.1
  11.6 2.4 broadcast_select_fusion
  14.0 0.9 copy-done
  15.1 215.0 %all-reduce.5.cloned.1.call-done = (bf16[2,2048,512]{2,1,0:T(8,128)(2,1)}, bf16[2,2048,512]{2,1,0:T(8,128)(2,1)}) async-done(((bf16[2,2048,512]{2,1,0:T(8,128)(2,1)}, bf16[2,2048,512]{2,1,0:T(8,128)(2,1)}), (bf16[2,2048,512]{2,1,0:T(8,128)(2,1)}, bf16[2,2048,512]{2,1,0:T(8,128)(2,1)})) %all-reduce.5.cloned.1.call-update) | async-done | bytes 8388624 | tf_op jit(solution)/shard_map/psum | solution.py:9
  230.0 3.3 dynamic-slice_select_fusion
  233.4 67.4 %all-reduce.7.cloned.1.call-done = (bf16[2,512,512]{2,1,0:T(8,128)(2,1)}, bf16[2,512,512]{2,1,0:T(8,128)(2,1)}) async-done(((bf16[2,512,512]{2,1,0:T(8,128)(2,1)}, bf16[2,512,512]{2,1,0:T(8,128)(2,1)}), (bf16[2,512,512]{2,1,0:T(8,128)(2,1)}, bf16[2,512,512]{2,1,0:T(8,128)(2,1)})) %all-reduce.7.cloned.1.call-update) | async-done | bytes 2097168 | tf_op jit(solution)/shard_map/psum | solution.py:9
  300.8 3.1 fusion
  304.1 1.3 fusion.1
  305.4 1.3 add_convert_fusion
  306.7 1.3 subtract_convert_fusion
  308.0 2.5 pad_maximum_fusion.1
  310.5 6.4 copy.10
  317.2 1.0 copy-done.4
  318.2 3.0 fusion.2
  321.2 1.3 fusion.3
  322.5 1.3 add_convert_fusion.1
  323.8 1.3 subtract_convert_fusion.1
  325.1 2.5 pad_maximum_fusion
  327.7 6.4 copy.8
  334.1 206.4 %reduce-scatter.9.cloned.1.call-done = bf16[64,1024]{1,0:T(8,128)(2,1)} async-done(((bf16[2048,1024]{1,0:T(8,128)(2,1)}), bf16[64,1024]{1,0:T(8,128)(2,1)}) %reduce-scatter.9.cloned.1.call-update) | async-done | bytes 131088
  540.5 1.1 copy.11
  541.7 222.6 %reduce-scatter.7.cloned.1.call-done = bf16[64,1024]{1,0:T(8,128)(2,1)} async-done(((bf16[2048,1024]{1,0:T(8,128)(2,1)}), bf16[64,1024]{1,0:T(8,128)(2,1)}) %reduce-scatter.7.cloned.1.call-update) | async-done | bytes 131088
  764.2 1.1 copy.9
  (23 shorter events, 2.9 us)
Async XLA Ops:
  6.5 223.5 %all-reduce.5.cloned.1.call-start = ((), (), s32[]{:S(2)}) async-start(), calls=%async_computation.4 | async-start | bytes 16777216 | tf_op jit(solution)/shard_map/psum | solution.py:9
  6.5 2.3 copy-start.3
  11.6 3.3 copy-start
  15.0 285.8 %all-reduce.7.cloned.1.call-start = ((), (), s32[]{:S(2)}) async-start(), calls=%async_computation.5 | async-start | bytes 4194304 | tf_op jit(solution)/shard_map/psum | solution.py:9
  233.3 307.1 %reduce-scatter.9.cloned.1.call-start = ((), (), s32[]{:S(2)}) async-start(), calls=%async_computation.3 | async-start | bytes 4325376
  300.8 3.1 copy-start.1
  300.8 3.3 copy-start.5
  316.9 1.2 copy-start.4
  317.0 447.3 %reduce-scatter.7.cloned.1.call-start = ((), (), s32[]{:S(2)}) async-start(), calls=%async_computation.2 | async-start | bytes 4325376
  318.2 3.0 copy-start.2
Sparse Core Ops, SparseCore 0:
  15.1 214.8 all-reduce.4
  233.5 67.2 all-reduce.6
  317.1 223.3 reduce-scatter.8
  544.7 219.4 reduce-scatter.6
where the time goes:
time: 773 us
  waiting for transfers between devices  711 us (92%)
  local copies, waits for them, and re-layouts  17.8 us (2%)
  other arithmetic  16 us (2%)
  matrix products  13.9 us (2%)
  between operations  13.3 us (2%)
    unnamed x6, waiting for transfers between devices  429 us
    psum x2, waiting for transfers between devices, from_root(): return lax.psum(kept, axis)  282 us
    unnamed x16, local copies, waits for them, and re-layouts  17 us
  transfers between devices with their start and end apart: 4, of which 4 were waited for; matrix products, arithmetic and copies ran while one was open for 2% of the time, Pallas kernels for 0%

commit v1 on v0

v1 whole, which is shorter than its diff:
```python
import functools

import jax
import jax.numpy as jnp
from jax import lax
from jax.experimental import pallas as pl
from jax.experimental.pallas import tpu as pltpu
from jax.sharding import PartitionSpec as P

MESH = pl.DeviceIdType.MESH
NY, NZ, NX = 4, 8, 4
WAVES = 4
LANES = 128
SPAN = 3


def wrap(index, size):
    return lax.rem(index + size, size)


class Chain:
    def __init__(self, n, me, neighbour, own, groups, send, recv, send_sem, recv_sem):
        self.n, self.me, self.neighbour, self.own, self.groups = n, me, neighbour, own, groups
        self.send, self.recv, self.send_sem, self.recv_sem = send, recv, send_sem, recv_sem
        self.started = []

    def half(self, side):
        size = self.groups // 2
        return pl.ds(size * side, size)

    def copy(self, side, step):
        if step == 0:
            cut = self.half(side)
            source, target = self.send.at[side, 0, cut], self.recv.at[side, 0, cut]
        else:
            source, target = self.send.at[side, step], self.recv.at[side, step]
        return pltpu.make_async_remote_copy(
            src_ref=source,
            dst_ref=target,
            send_sem=self.send_sem.at[side, step],
            recv_sem=self.recv_sem.at[side, step],
            device_id=self.neighbour(1 - 2 * side),
            device_id_type=MESH,
        )

    def step(self, step):
        for side in range(2):
            away = self.n // 2 - step
            dest = wrap(self.me + (1 - 2 * side) * away, self.n)
            size = self.groups // 2
            halves = (side, 1 - side) if step else (side,)
            if step:
                self.copy(side, step - 1).wait_recv()
            for part in halves:
                with_received = step > 1 or (step == 1 and part == side)

                def block(g, _, part=part, with_received=with_received, dest=dest, side=side):
                    at = part * size + g
                    value = self.own(dest, at)
                    if with_received:
                        value = value + self.recv[side, step - 1, at].astype(jnp.float32)
                    self.send[side, step, at] = value.astype(jnp.bfloat16)
                    return _

                lax.fori_loop(0, size, block, 0)
            copy = self.copy(side, step)
            copy.start()
            self.started.append(copy)

    def finish(self, put):
        last = self.n // 2 - 1
        for side in range(2):
            self.copy(side, last).wait_recv()

        def block(g, _):
            value = self.own(self.me, g)
            for side in range(2):
                value = value + self.recv[side, last, g].astype(jnp.float32)
            put(g, value)
            return _

        lax.fori_loop(0, self.groups, block, 0)

    def drain(self):
        for copy in self.started:
            copy.wait_send()


def kernel(
    raw_ref, occ_ref, exp_ref, out_ref,
    raw, factor, mine, land, rhs, part, summed,
    z_send, z_recv, x_send, x_recv, zx_send, zx_recv, xz_send, xz_recv,
    raw_sem, root_sem, land_sem, pass_sem,
    z_ss, z_rs, x_ss, x_rs, zx_ss, zx_rs, xz_ss, xz_rs,
):
    row, col = lax.axis_index("row"), lax.axis_index("col")
    y, core, z, x = row // 2, row % 2, col // NX, col % NX

    def device(y, core, z, x):
        return (wrap(y, NY) * 2 + core, wrap(z, NZ) * NX + wrap(x, NX))

    def along_z(step):
        return device(y, core, z + step, x)

    def along_x(step):
        return device(y, core, z, x + step)

    def along_y(step):
        return device(y + step, core, z, x)

    other = device(y, 1 - core, z, x)
    fetches = [
        pltpu.make_async_copy(
            raw_ref.at[:, :, :, :, pl.ds(LANES * q, LANES)],
            raw.at[:, :, :, :, pl.ds(LANES * q, LANES)],
            raw_sem.at[q],
        )
        for q in range(WAVES)
    ]
    for fetch in fetches:
        fetch.start()

    barrier = pltpu.get_barrier_semaphore()
    for peer in (along_z(1), along_z(-1), along_x(1), along_x(-1), along_y(1), along_y(-1), other):
        pl.semaphore_signal(barrier, inc=1, device_id=peer, device_id_type=MESH)
    expected = jnp.int32(7)
    is_root = [col == p * (NZ * NX // 2) for p in range(2)]
    is_first = row == z
    for p in range(2):
        for j in range(NX):
            target = row * NX + j
            needed = jnp.logical_and(is_root[p], target != col)
            expected = expected + needed.astype(jnp.int32)

            @pl.when(needed)
            def _(target=target):
                pl.semaphore_signal(barrier, inc=1, device_id=(row, target), device_id_type=MESH)

        needed = jnp.logical_and(is_first, jnp.logical_not(is_root[p]))
        expected = expected + needed.astype(jnp.int32)

        @pl.when(needed)
        def _(p=p):
            pl.semaphore_signal(
                barrier, inc=1, device_id=(row, jnp.int32(p * (NZ * NX // 2))), device_id_type=MESH
            )

    exponent = exp_ref[...]
    scale = jnp.full(exponent.shape, 1.0, jnp.float32)
    for power in (-2, -1, 1, 2):
        scale = jnp.where(exponent == power, jnp.float32(2.0**power), scale)
    scaled = occ_ref[...].astype(jnp.float32) * scale
    for tile in range(NZ // 2):
        factor[tile] = scaled[tile : tile + 1]

    def root_copy(p, q, j):
        return pltpu.make_async_remote_copy(
            src_ref=mine.at[pl.ds(2 * j, 2), :, :, pl.ds(2 * LANES * q, 2 * LANES)],
            dst_ref=land.at[p, q],
            send_sem=root_sem.at[q, j],
            recv_sem=land_sem.at[p, q],
            device_id=(row, row * NX + j),
            device_id_type=MESH,
        )

    def stay_copy(p, q):
        return pltpu.make_async_copy(
            mine.at[pl.ds(0, 2), :, :, pl.ds(2 * LANES * q, 2 * LANES)], land.at[p, q], land_sem.at[p, q]
        )

    for q in range(WAVES):
        fetches[q].wait()

        def decode(zd, _, q=q):
            f = factor[zd // 2, :, LANES * q : LANES * (q + 1)]
            for half in range(2):
                value = raw[half, zd, :, :, LANES * q : LANES * (q + 1)].astype(jnp.float32)
                start = 2 * LANES * q + LANES * half
                mine[zd, :, :, start : start + LANES] = (value * f[None]).astype(jnp.bfloat16)
            return _

        lax.fori_loop(0, NZ, decode, 0)
        if q == 0:
            pl.semaphore_wait(barrier, expected)
        for p in range(2):
            for j in range(NX):
                own = row * NX + j == col

                @pl.when(jnp.logical_and(is_root[p], jnp.logical_not(own)))
                def _(p=p, q=q, j=j):
                    root_copy(p, q, j).start()

            @pl.when(jnp.logical_and(is_root[p], is_first))
            def _(p=p, q=q):
                stay_copy(p, q).start()

    match = core == z % 2
    dy = wrap(y - z // 2, NY)

    def passes(p, q):
        forward = jnp.logical_or(dy == 0, dy == (1 if q % 2 == 0 else NY))
        backward = jnp.logical_or(dy == 0, dy == (NY - 1 if q % 2 == 1 else NY))
        for slot, (needed, peer) in enumerate(
            ((forward, along_y(1)), (backward, along_y(-1)), (dy >= 0, other))
        ):
            copy = pltpu.make_async_remote_copy(
                src_ref=land.at[p, q],
                dst_ref=land.at[p, q],
                send_sem=pass_sem.at[p, q, slot],
                recv_sem=land_sem.at[p, q],
                device_id=peer,
                device_id_type=MESH,
            )
            yield jnp.logical_and(match, needed), copy

    def arrive(p, q):
        pltpu.make_async_copy(land.at[p, q], land.at[p, q], land_sem.at[p, q]).wait()
        for needed, copy in passes(p, q):

            @pl.when(needed)
            def _(copy=copy):
                copy.start()

    def build(p, q):
        for k in range(4):
            block = land[p, q, k // 2, 2 * (k % 2) : 2 * (k % 2) + 2].reshape(LANES, 2 * LANES)
            real, imag = block[:, :LANES], block[:, LANES:]
            at = 2 * LANES * k
            rhs[p, at : at + LANES, :] = block
            rhs[p, at + LANES : at + 2 * LANES, :LANES] = -imag
            rhs[p, at + LANES : at + 2 * LANES, LANES:] = real

    def product(p, rows):
        return jnp.dot(rows.reshape(4 * 64, 8 * LANES), rhs[p], preferred_element_type=jnp.float32)

    def multiply_z(slot, start, count):
        def block(k, _):
            zd = wrap(z + NZ // 2 + k, NZ)
            part[slot, 0, zd] = product(0, mine[zd]).reshape(4, 64, 2 * LANES)
            return _

        lax.fori_loop(start, start + count, block, 0)

    def multiply_x(slot, start, count):
        def block(k, _):
            xd = wrap(x + NX // 2 + k // 2, NX)
            rows = pl.ds(4 * (k % 2), 4)
            part[slot, 1, rows, xd] = product(1, mine[rows, xd]).reshape(4, 64, 2 * LANES)
            return _

        lax.fori_loop(start, start + count, block, 0)

    def chains(w):
        slot = w % 2
        first_z = Chain(
            NZ, z, along_z, lambda d, g: part[slot, 0, d, g], NX,
            z_send.at[w], z_recv.at[w], z_ss.at[w], z_rs.at[w],
        )
        first_x = Chain(
            NX, x, along_x, lambda d, g: part[slot, 1, g, d], NZ,
            x_send.at[w], x_recv.at[w], x_ss.at[w], x_rs.at[w],
        )
        then_x = Chain(
            NX, x, along_x, lambda d, g: summed[slot, 0, d, g], 2,
            zx_send.at[w], zx_recv.at[w], zx_ss.at[w], zx_rs.at[w],
        )
        then_z = Chain(
            NZ, z, along_z, lambda d, g: summed[slot, 1, d, g], 2,
            xz_send.at[w], xz_recv.at[w], xz_ss.at[w], xz_rs.at[w],
        )
        return first_z, first_x, then_x, then_z

    all_chains = [chains(w) for w in range(WAVES)]

    def keep(slot, which):
        def put(g, value):
            summed[slot, which, g] = value.reshape(2, 32, 2 * LANES)

        return put

    def result(p, w):
        def put(g, value):
            value = value.astype(jnp.bfloat16)
            for half in range(2):
                out_ref[p, half, pl.ds(pl.multiple_of(32 * g, 32), 32), LANES * w : LANES * (w + 1)] = value[
                    :, LANES * half : LANES * (half + 1)
                ]

        return put

    def run(w, k):
        first_z, first_x, then_x, then_z = all_chains[w]
        slot = w % 2
        if k == 0:
            arrive(0, w)
            arrive(1, w)
            build(0, w)
            multiply_z(slot, 0, 1)
            first_z.step(0)
            build(1, w)
            multiply_x(slot, 0, 2)
            first_x.step(0)
            multiply_z(slot, 1, 7)
            multiply_x(slot, 2, 6)
        if 1 <= k <= 3:
            first_z.step(k)
        if k == 1:
            first_x.step(1)
        if k == 2:
            first_x.finish(keep(slot, 1))
        if 2 <= k <= 5:
            then_z.step(k - 2)
        if k == 4:
            first_z.finish(keep(slot, 0))
        if 4 <= k <= 5:
            then_x.step(k - 4)
        if k == 6:
            then_x.finish(result(0, w))
            then_z.finish(result(1, w))

    for t in range(SPAN * (WAVES - 1) + 7):
        for w in range(WAVES):
            if 0 <= t - SPAN * w <= 6:
                run(w, t - SPAN * w)

    for group in all_chains:
        for chain in group:
            chain.drain()
    for p in range(2):
        for q in range(WAVES):
            for needed, copy in passes(p, q):

                @pl.when(needed)
                def _(copy=copy):
                    copy.wait_send()

            for j in range(NX):

                @pl.when(jnp.logical_and(is_root[p], row * NX + j != col))
                def _(p=p, q=q, j=j):
                    root_copy(p, q, j).wait_send()


def on_device(raw_blocks, occupancy, exponent):
    bf16, f32 = jnp.bfloat16, jnp.float32
    dma = pltpu.SemaphoreType.DMA
    n = 2 * LANES
    return pl.pallas_call(
        kernel,
        out_shape=jax.ShapeDtypeStruct((2, 2, 64, 512), bf16),
        in_specs=[
            pl.BlockSpec(memory_space=pl.ANY),
            pl.BlockSpec(memory_space=pltpu.VMEM),
            pl.BlockSpec(memory_space=pltpu.VMEM),
        ],
        out_specs=pl.BlockSpec(memory_space=pltpu.VMEM),
        scratch_shapes=[
            pltpu.VMEM((2, NZ, NX, 64, 512), bf16),
            pltpu.VMEM((4, 1, 512), f32),
            pltpu.VMEM((NZ, NX, 64, 1024), bf16),
            pltpu.VMEM((2, WAVES, 2, NX, 64, n), bf16),
            pltpu.VMEM((2, 1024, n), bf16),
            pltpu.VMEM((2, 2, NZ, NX, 64, n), f32),
            pltpu.VMEM((2, 2, NZ, 2, 32, n), f32),
            pltpu.VMEM((WAVES, 2, NZ // 2, NX, 64, n), bf16),
            pltpu.VMEM((WAVES, 2, NZ // 2, NX, 64, n), bf16),
            pltpu.VMEM((WAVES, 2, NX // 2, NZ, 64, n), bf16),
            pltpu.VMEM((WAVES, 2, NX // 2, NZ, 64, n), bf16),
            pltpu.VMEM((WAVES, 2, NX // 2, 2, 32, n), bf16),
            pltpu.VMEM((WAVES, 2, NX // 2, 2, 32, n), bf16),
            pltpu.VMEM((WAVES, 2, NZ // 2, 2, 32, n), bf16),
            pltpu.VMEM((WAVES, 2, NZ // 2, 2, 32, n), bf16),
            dma((WAVES,)),
            dma((WAVES, NX)),
            dma((2, WAVES)),
            dma((2, WAVES, 3)),
            dma((WAVES, 2, NZ // 2)),
            dma((WAVES, 2, NZ // 2)),
            dma((WAVES, 2, NX // 2)),
            dma((WAVES, 2, NX // 2)),
            dma((WAVES, 2, NX // 2)),
            dma((WAVES, 2, NX // 2)),
            dma((WAVES, 2, NZ // 2)),
            dma((WAVES, 2, NZ // 2)),
        ],
        compiler_params=pltpu.CompilerParams(
            collective_id=0, has_side_effects=True, vmem_limit_bytes=56 * 2**20
        ),
    )(raw_blocks.reshape(2, NZ, NX, 64, 512), occupancy, exponent)


def solution(mesh):
    placed = (P(None, "row", "col"), P("row", "col"), P("row", "col"))
    return jax.shard_map(
        on_device,
        mesh=mesh,
        in_specs=placed,
        out_specs=P(None, None, ("row", "col"), None),
        check_vma=False,
    )
```

time: 773 us -> 216 us (0.28)
  waiting for transfers between devices: 711 us -> 0 us
  Pallas kernels: 0 us -> 212 us
  other arithmetic: 16 us -> 0 us
  local copies, waits for them, and re-layouts: 17.8 us -> 2.98 us
  matrix products: 13.9 us -> 0 us
  between operations: 13.3 us -> 0.01 us
    unnamed x6 -> x0, waiting for transfers between devices: 429 us -> none
    psum x2 -> x0, waiting for transfers between devices: 282 us -> none  [from_root(): return lax.psum(kept, axis)]
    pallas_call x0 -> x1, Pallas kernels: none -> 212 us  [on_device(): pl.pallas_call(kernel, out_shape=jax.ShapeDtypeStruct((2, 2, 64, 512), bf...]
    unnamed x16 -> x2, local copies, waits for them, and re-layouts: 17 us -> 2.98 us
    dot_general x8 -> x0, matrix products: 13.9 us -> none  [the longest x2 6.14 us: complex_term(): jnp.dot(decoded[0], slab_piece[1], preferred_element_type=jnp.float32)]
    select_n x3 -> x0, other arithmetic: 8.47 us -> none  [from_root(): jnp.where(lax.axis_index(axis) == source, value, 0).astype(value.dtype)]
  transfers between devices with their start and end apart: 4 -> 0, of which waited for: 4 -> 0; matrix products, arithmetic and copies ran while one was open for 2% -> 0% of each run, Pallas kernels for 0% -> 0%
where the time goes in v1:
time: 216 us; the launch traced here: 215 us
  Pallas kernels  212 us (98%)
  local copies, waits for them, and re-layouts  2.98 us (1%)
    pallas_call x1, Pallas kernels, on_device(): pl.pallas_call(kernel, out_shape=jax.ShapeDtypeStruct((2, 2, 64, 512), bf...  212 us

profile of v1, /device:TPU:8, one launch (start us, length us, event | category | flops | bytes accessed | tf_op | source)
XLA Modules:
  0.0 215.4 jit_solution(298494249336698528)
XLA Ops:
  0.0 1.3 copy.4.exp_ref
  1.3 212.4 %shard_map.37 = bf16[2,2,64,512]{3,2,1,0:T(8,128)(2,1)} custom-call(bf16[2,8,4,64,512]{4,3,2,1,0:T(8,128)(2,1)} %bitcast.1, s32[4,512]{1,0:T(4,128)} %occ_ref.1, s32[4,1]{1,0:T(4,128)} %copy.4.exp_ref), custom_call_target="tpu_custom_call" | custom-call | tf_op jit(solution)/shard_map/pallas_call | solution.py:348
  213.7 1.7 copy.6

commit v2 on v1

--- a/solution.py
+++ b/solution.py
@@ -11,7 +11,8 @@
 NY, NZ, NX = 4, 8, 4
 WAVES = 4
 LANES = 128
-SPAN = 3
+SPAN = 2
+FAR = 6
 
 
 def wrap(index, size):
@@ -88,9 +89,9 @@
 
 def kernel(
     raw_ref, occ_ref, exp_ref, out_ref,
-    raw, factor, mine, land, rhs, part, summed,
+    raw, factor, mine, land, hold, rhs, part, summed,
     z_send, z_recv, x_send, x_recv, zx_send, zx_recv, xz_send, xz_recv,
-    raw_sem, root_sem, land_sem, pass_sem,
+    raw_sem, root_sem, land_sem, hold_sem, relay_sem, pass_sem,
     z_ss, z_rs, x_ss, x_rs, zx_ss, zx_rs, xz_ss, xz_rs,
 ):
     row, col = lax.axis_index("row"), lax.axis_index("col")
@@ -124,49 +125,104 @@
     for peer in (along_z(1), along_z(-1), along_x(1), along_x(-1), along_y(1), along_y(-1), other):
         pl.semaphore_signal(barrier, inc=1, device_id=peer, device_id_type=MESH)
     expected = jnp.int32(7)
-    is_root = [col == p * (NZ * NX // 2) for p in range(2)]
-    is_first = row == z
+    both = jnp.logical_and
+    root_col = [p * (NZ * NX // 2) for p in range(2)]
+    is_root = [col == c for c in root_col]
+    odd = x % 2 == 1
+
+    def distance(p, plane):
+        return wrap(plane - p * (NZ // 2), NZ)
+
+    def moved(p, plane):
+        d = distance(p, plane)
+        return jnp.logical_or(jnp.logical_or(d == 3, d == 4), d == 7)
+
+    prior = wrap(row - 2, NZ)
+    here = [distance(p, row) == 0 for p in range(2)]
+    direct = [both(is_root[p], jnp.logical_not(moved(p, row))) for p in range(2)]
+    relay_x = [
+        both(jnp.logical_or(col == root_col[p] + 1, col == root_col[p] + 3), jnp.logical_not(here[p]))
+        for p in range(2)
+    ]
+    relay_n = [both(col == root_col[p] + 3, here[p]) for p in range(2)]
+    relay_y = [both(is_root[p], moved(p, prior)) for p in range(2)]
+    match = core == z % 2
+    dy = [wrap(y - z // 2 - both(jnp.logical_not(odd), moved(p, z)).astype(jnp.int32), NY) for p in range(2)]
+    first = [both(match, dy[p] == 0) for p in range(2)]
+
+    greet = []
     for p in range(2):
-        for j in range(NX):
-            target = row * NX + j
-            needed = jnp.logical_and(is_root[p], target != col)
-            expected = expected + needed.astype(jnp.int32)
-
-            @pl.when(needed)
-            def _(target=target):
-                pl.semaphore_signal(barrier, inc=1, device_id=(row, target), device_id_type=MESH)
-
-        needed = jnp.logical_and(is_first, jnp.logical_not(is_root[p]))
+        greet.append((both(direct[p], jnp.logical_not(here[p])), row * NX))
+        greet.append((direct[p], row * NX + 2))
+        greet.append((relay_x[p], row * NX + x))
+        greet.append((relay_y[p], prior * NX))
+        greet.append((relay_y[p], prior * NX + 2))
+        near = both(distance(p, z) == 0, x != 2)
+        greet.append((both(first[p], jnp.logical_not(near)), root_col[p] + jnp.where(odd, x, 0)))
+    for needed, peer in greet:
         expected = expected + needed.astype(jnp.int32)
 
         @pl.when(needed)
-        def _(p=p):
-            pl.semaphore_signal(
-                barrier, inc=1, device_id=(row, jnp.int32(p * (NZ * NX // 2))), device_id_type=MESH
+        def _(peer=peer):
+            pl.semaphore_signal(barrier, inc=1, device_id=(row, peer), device_id_type=MESH)
+
+    present = occ_ref[...].astype(jnp.float32)
+    for tile in range(NZ // 2):
+        exponent = exp_ref[tile, 0]
+        scale = jnp.float32(1.0)
+        for power in (-2, -1, 1, 2):
+            scale = jnp.where(exponent == power, jnp.float32(2.0**power), scale)
+        factor[tile] = present[tile : tile + 1] * scale
+
+    def piece(j, q, h):
+        return mine.at[2 * j + h, :, :, pl.ds(2 * LANES * q, 2 * LANES)]
+
+    def give(source, target, send_sem, recv_sem, peer):
+        return pltpu.make_async_remote_copy(
+            src_ref=source, dst_ref=target, send_sem=send_sem, recv_sem=recv_sem,
+            device_id=peer, device_id_type=MESH,
+        )
+
+    def root_copies(p, q, h):
+        def to(j, target, recv_sem, peer):
+            return give(piece(j, q, h), target, root_sem.at[q, h, j], recv_sem, peer)
+
+        held = hold.at[0, q, h], hold_sem.at[0, q, h]
+        held_too = hold.at[1, q, h], hold_sem.at[1, q, h]
+        landed = land.at[p, 2 * q + h], land_sem.at[p, 2 * q + h]
+        far = both(is_root[p], jnp.logical_not(here[p]))
+        close = both(is_root[p], here[p])
+        for j in (1, 3):
+            peer = (row, jnp.int32(root_col[p] + j))
+            yield far, to(j, *held, peer)
+            yield close, to(j, *landed, peer)
+        shift = both(is_root[p], moved(p, row))
+        yield both(direct[p], jnp.logical_not(here[p])), to(0, *landed, (row, row * NX))
+        yield shift, to(0, *held, along_y(1))
+        yield both(direct[p], jnp.logical_not(here[p])), to(2, *landed, (row, row * NX + 2))
+        if h == 0:
+            yield close, to(2, *landed, (row, row * NX + 2))
+        else:
+            yield close, to(2, *held_too, (row, jnp.int32(root_col[p] + 3)))
+        yield shift, to(2, *held_too, along_y(1))
+
+    def relay_copies(p, q, h):
+        for needed, slot, target in (
+            (relay_x[p], 0, row * NX + x),
+            (relay_y[p], 0, prior * NX),
+            (relay_y[p], 1, prior * NX + 2),
+            (relay_n[p], 1, row * NX + 2),
+        ):
+            if needed is relay_n[p] and h == 0:
+                continue
+            kind = 1 if needed is relay_y[p] else 0
+            yield needed, slot, give(
+                hold.at[slot, q, h], land.at[p, 2 * q + h], relay_sem.at[kind, slot, q, h], land_sem.at[p, 2 * q + h],
+                (row, target),
             )
 
-    exponent = exp_ref[...]
-    scale = jnp.full(exponent.shape, 1.0, jnp.float32)
-    for power in (-2, -1, 1, 2):
-        scale = jnp.where(exponent == power, jnp.float32(2.0**power), scale)
-    scaled = occ_ref[...].astype(jnp.float32) * scale
-    for tile in range(NZ // 2):
-        factor[tile] = scaled[tile : tile + 1]
-
-    def root_copy(p, q, j):
-        return pltpu.make_async_remote_copy(
-            src_ref=mine.at[pl.ds(2 * j, 2), :, :, pl.ds(2 * LANES * q, 2 * LANES)],
-            dst_ref=land.at[p, q],
-            send_sem=root_sem.at[q, j],
-            recv_sem=land_sem.at[p, q],
-            device_id=(row, row * NX + j),
-            device_id_type=MESH,
-        )
-
-    def stay_copy(p, q):
-        return pltpu.make_async_copy(
-            mine.at[pl.ds(0, 2), :, :, pl.ds(2 * LANES * q, 2 * LANES)], land.at[p, q], land_sem.at[p, q]
-        )
+    def stay_copy(p, q, h):
+        return pltpu.make_async_copy(piece(0, q, h), land.at[p, 2 * q + h], land_sem.at[p, 2 * q + h])
 
     for q in range(WAVES):
         fetches[q].wait()
@@ -183,47 +239,54 @@
         if q == 0:
             pl.semaphore_wait(barrier, expected)
         for p in range(2):
-            for j in range(NX):
-                own = row * NX + j == col
-
-                @pl.when(jnp.logical_and(is_root[p], jnp.logical_not(own)))
-                def _(p=p, q=q, j=j):
-                    root_copy(p, q, j).start()
-
-            @pl.when(jnp.logical_and(is_root[p], is_first))
-            def _(p=p, q=q):
-                stay_copy(p, q).start()
-
-    match = core == z % 2
-    dy = wrap(y - z // 2, NY)
-
-    def passes(p, q):
-        forward = jnp.logical_or(dy == 0, dy == (1 if q % 2 == 0 else NY))
-        backward = jnp.logical_or(dy == 0, dy == (NY - 1 if q % 2 == 1 else NY))
-        for slot, (needed, peer) in enumerate(
-            ((forward, along_y(1)), (backward, along_y(-1)), (dy >= 0, other))
-        ):
-            copy = pltpu.make_async_remote_copy(
-                src_ref=land.at[p, q],
-                dst_ref=land.at[p, q],
-                send_sem=pass_sem.at[p, q, slot],
-                recv_sem=land_sem.at[p, q],
-                device_id=peer,
-                device_id_type=MESH,
-            )
-            yield jnp.logical_and(match, needed), copy
-
-    def arrive(p, q):
-        pltpu.make_async_copy(land.at[p, q], land.at[p, q], land_sem.at[p, q]).wait()
-        for needed, copy in passes(p, q):
-
-            @pl.when(needed)
-            def _(copy=copy):
-                copy.start()
+            for h in range(2):
+                for needed, copy in root_copies(p, q, h):
+
+                    @pl.when(needed)
+                    def _(copy=copy):
+                        copy.start()
+
+                @pl.when(both(is_root[p], here[p]))
+                def _(p=p, q=q, h=h):
+                    stay_copy(p, q, h).start()
+
+    def relay(q, h):
+        for p in range(2):
+            for needed, slot, copy in relay_copies(p, q, h):
+
+                @pl.when(needed)
+                def _(copy=copy, slot=slot):
+                    pltpu.make_async_copy(hold.at[slot, q, h], hold.at[slot, q, h], hold_sem.at[slot, q, h]).wait()
+                    copy.start()
+
+    def passes(p, i):
+        onward, last = (1, NY - 1) if p == 0 else (-1, 1)
+        for slot, (needed, peer) in enumerate(((dy[p] != last, along_y(onward)), (dy[p] >= 0, other))):
+            copy = give(land.at[p, i], land.at[p, i], pass_sem.at[p, i, slot], land_sem.at[p, i], peer)
+            yield both(match, needed), copy
+
+    def hops(p):
+        even = jnp.where(distance(p, z) == 0, jnp.where(x == 0, 0, 2), jnp.where(moved(p, z), 2, 1))
+        at_first = jnp.where(odd, jnp.where(distance(p, z) == 0, 1, 2), even)
+        return at_first + (dy[p] if p == 0 else wrap(-dy[p], NY)) + 1 - match.astype(jnp.int32)
+
+    away = [hops(p) for p in range(2)]
+
+    def arrive(p, tick):
+        i = tick - away[p]
+
+        @pl.when(both(i >= 0, i < 2 * WAVES))
+        def _():
+            pltpu.make_async_copy(land.at[p, i], land.at[p, i], land_sem.at[p, i]).wait()
+            for needed, copy in passes(p, i):
+
+                @pl.when(needed)
+                def _(copy=copy):
+                    copy.start()
 
     def build(p, q):
         for k in range(4):
-            block = land[p, q, k // 2, 2 * (k % 2) : 2 * (k % 2) + 2].reshape(LANES, 2 * LANES)
+            block = land[p, 2 * q + k // 2, 2 * (k % 2) : 2 * (k % 2) + 2].reshape(LANES, 2 * LANES)
             real, imag = block[:, :LANES], block[:, LANES:]
             at = 2 * LANES * k
             rhs[p, at : at + LANES, :] = block
@@ -231,27 +294,29 @@
             rhs[p, at + LANES : at + 2 * LANES, LANES:] = real
 
     def product(p, rows):
-        return jnp.dot(rows.reshape(4 * 64, 8 * LANES), rhs[p], preferred_element_type=jnp.float32)
+        return jnp.dot(rows.reshape(8 * 64, 8 * LANES), rhs[p], preferred_element_type=jnp.float32)
 
     def multiply_z(slot, start, count):
         def block(k, _):
-            zd = wrap(z + NZ // 2 + k, NZ)
-            part[slot, 0, zd] = product(0, mine[zd]).reshape(4, 64, 2 * LANES)
+            pair = [wrap(z + NZ // 2 + 2 * k + i, NZ) for i in range(2)]
+            rows = jnp.concatenate([mine[zd] for zd in pair], axis=0)
+            terms = product(0, rows).reshape(2, 4, 64, 2 * LANES)
+            for i, zd in enumerate(pair):
+                part[slot, 0, zd] = terms[i]
             return _
 
         lax.fori_loop(start, start + count, block, 0)
 
     def multiply_x(slot, start, count):
         def block(k, _):
-            xd = wrap(x + NX // 2 + k // 2, NX)
-            rows = pl.ds(4 * (k % 2), 4)
-            part[slot, 1, rows, xd] = product(1, mine[rows, xd]).reshape(4, 64, 2 * LANES)
+            xd = wrap(x + NX // 2 + k, NX)
+            part[slot, 1, :, xd] = product(1, mine[:, xd]).reshape(8, 64, 2 * LANES)
             return _
 
         lax.fori_loop(start, start + count, block, 0)
 
     def chains(w):
-        slot = w % 2
+        slot = w
         first_z = Chain(
             NZ, z, along_z, lambda d, g: part[slot, 0, d, g], NX,
             z_send.at[w], z_recv.at[w], z_ss.at[w], z_rs.at[w],
@@ -288,20 +353,22 @@
 
         return put
 
+    def heads(w):
+        first_z, first_x, _, _ = all_chains[w]
+        build(0, w)
+        multiply_z(w, 0, 1)
+        first_z.step(0)
+        build(1, w)
+        multiply_x(w, 0, 1)
+        first_x.step(0)
+
+    def rest(w):
+        multiply_z(w, 1, 3)
+        multiply_x(w, 1, 3)
+
     def run(w, k):
         first_z, first_x, then_x, then_z = all_chains[w]
-        slot = w % 2
-        if k == 0:
-            arrive(0, w)
-            arrive(1, w)
-            build(0, w)
-            multiply_z(slot, 0, 1)
-            first_z.step(0)
-            build(1, w)
-            multiply_x(slot, 0, 2)
-            first_x.step(0)
-            multiply_z(slot, 1, 7)
-            multiply_x(slot, 2, 6)
+        slot = w
         if 1 <= k <= 3:
             first_z.step(k)
         if k == 1:
@@ -318,27 +385,34 @@
             then_x.finish(result(0, w))
             then_z.finish(result(1, w))
 
-    for t in range(SPAN * (WAVES - 1) + 7):
+    for tick in range(FAR + SPAN * (WAVES - 1) + 8):
+        if 1 <= tick <= 2 * WAVES:
+            relay((tick - 1) // 2, (tick - 1) % 2)
+        if tick < 2 * WAVES + FAR:
+            for p in range(2):
+                arrive(p, tick)
         for w in range(WAVES):
-            if 0 <= t - SPAN * w <= 6:
-                run(w, t - SPAN * w)
+            k = tick - FAR - 1 - SPAN * w
+            if k == 0:
+                heads(w)
+            if 1 <= k <= 6:
+                run(w, k)
+            if k == 0:
+                rest(w)
 
     for group in all_chains:
         for chain in group:
             chain.drain()
     for p in range(2):
         for q in range(WAVES):
-            for needed, copy in passes(p, q):
-
-                @pl.when(needed)
-                def _(copy=copy):
-                    copy.wait_send()
-
-            for j in range(NX):
-
-                @pl.when(jnp.logical_and(is_root[p], row * NX + j != col))
-                def _(p=p, q=q, j=j):
-                    root_copy(p, q, j).wait_send()
+            for h in range(2):
+                sent = [*root_copies(p, q, h), *passes(p, 2 * q + h)]
+                sent += [(needed, copy) for needed, _, copy in relay_copies(p, q, h)]
+                for needed, copy in sent:
+
+                    @pl.when(needed)
+                    def _(copy=copy):
+                        copy.wait_send()
 
 
 def on_device(raw_blocks, occupancy, exponent):
@@ -351,17 +425,18 @@
         in_specs=[
             pl.BlockSpec(memory_space=pl.ANY),
             pl.BlockSpec(memory_space=pltpu.VMEM),
-            pl.BlockSpec(memory_space=pltpu.VMEM),
+            pl.BlockSpec(memory_space=pltpu.SMEM),
         ],
         out_specs=pl.BlockSpec(memory_space=pltpu.VMEM),
         scratch_shapes=[
             pltpu.VMEM((2, NZ, NX, 64, 512), bf16),
             pltpu.VMEM((4, 1, 512), f32),
             pltpu.VMEM((NZ, NX, 64, 1024), bf16),
+            pltpu.VMEM((2, 2 * WAVES, NX, 64, n), bf16),
             pltpu.VMEM((2, WAVES, 2, NX, 64, n), bf16),
             pltpu.VMEM((2, 1024, n), bf16),
-            pltpu.VMEM((2, 2, NZ, NX, 64, n), f32),
-            pltpu.VMEM((2, 2, NZ, 2, 32, n), f32),
+            pltpu.VMEM((WAVES, 2, NZ, NX, 64, n), f32),
+            pltpu.VMEM((WAVES, 2, NZ, 2, 32, n), f32),
             pltpu.VMEM((WAVES, 2, NZ // 2, NX, 64, n), bf16),
             pltpu.VMEM((WAVES, 2, NZ // 2, NX, 64, n), bf16),
             pltpu.VMEM((WAVES, 2, NX // 2, NZ, 64, n), bf16),
@@ -371,9 +446,11 @@
             pltpu.VMEM((WAVES, 2, NZ // 2, 2, 32, n), bf16),
             pltpu.VMEM((WAVES, 2, NZ // 2, 2, 32, n), bf16),
             dma((WAVES,)),
-            dma((WAVES, NX)),
-            dma((2, WAVES)),
-            dma((2, WAVES, 3)),
+            dma((WAVES, 2, NX)),
+            dma((2, 2 * WAVES)),
+            dma((2, WAVES, 2)),
+            dma((2, 2, WAVES, 2)),
+            dma((2, 2 * WAVES, 2)),
             dma((WAVES, 2, NZ // 2)),
             dma((WAVES, 2, NZ // 2)),
             dma((WAVES, 2, NX // 2)),
@@ -384,7 +461,7 @@
             dma((WAVES, 2, NZ // 2)),
         ],
         compiler_params=pltpu.CompilerParams(
-            collective_id=0, has_side_effects=True, vmem_limit_bytes=56 * 2**20
+            collective_id=0, has_side_effects=True, vmem_limit_bytes=60 * 2**20
         ),
     )(raw_blocks.reshape(2, NZ, NX, 64, 512), occupancy, exponent)
 

time: 216 us -> 128 us (0.59)
  Pallas kernels: 212 us -> 125 us
    pallas_call x1, Pallas kernels: 212 us -> 125 us  [on_device(): pl.pallas_call(kernel, out_shape=jax.ShapeDtypeStruct((2, 2, 64, 512), bf...]
where the time goes in v2:
time: 128 us
  Pallas kernels  125 us (98%)
  local copies, waits for them, and re-layouts  2.98 us (2%)
    pallas_call x1, Pallas kernels, on_device(): pl.pallas_call(kernel, out_shape=jax.ShapeDtypeStruct((2, 2, 64, 512), bf...  125 us
    unnamed x2, local copies, waits for them, and re-layouts  2.98 us

profile of v2, /device:TPU:8, one launch (start us, length us, event | category | flops | bytes accessed | tf_op | source)
XLA Modules:
  0.0 127.6 jit_solution(15745735601475832180)
XLA Ops:
  0.0 1.3 %copy.4.exp_ref = s32[4,1]{1,0:T(4,128)} copy(s32[4,1]{0,1:T(1,128)} %param.5) | data formatting | bytes 32 | tf_op args[2]
  1.3 124.6 %shard_map.37 = bf16[2,2,64,512]{3,2,1,0:T(8,128)(2,1)} custom-call(bf16[2,8,4,64,512]{4,3,2,1,0:T(8,128)(2,1)} %bitcast.1, s32[4,512]{1,0:T(4,128)} %occ_ref.1, s32[4,1]{1,0:T(4,128)} %copy.4.exp_ref), custom_call_target="tpu_custom_call" | custom-call | tf_op jit(solution)/shard_map/pallas_call | solution.py:422
  126.0 1.7 %copy.6 = bf16[2,2,64,512]{3,2,1,0:T(8,128)(2,1)} copy(bf16[2,2,64,512]{3,2,1,0:T(8,128)(2,1)} %shard_map.37) | data formatting | bytes 524288

commit v3 on v2

--- a/solution.py
+++ b/solution.py
@@ -11,8 +11,17 @@
 NY, NZ, NX = 4, 8, 4
 WAVES = 4
 LANES = 128
-SPAN = 2
-FAR = 6
+PACE = 2
+HOP = 3
+DEEP = 2
+ORDER = (
+    "k0", "k1", "k2", "k3", "k4", "k5", "k6", "k7", "k8", "k9", "k10", "k11", "k12", "k13", "k14", "k15",
+    "k16", "k17", "0H", "0M", "k18", "1H", "1M", "k19", "k20", "0s1", "k21", "3H", "2H", "2M", "k22", "3M",
+    "k23", "0s2", "k24", "1s1", "2s1", "k25", "3s1", "4H", "4M", "k26", "5H", "k27", "5M", "k28", "0s3", "k29",
+    "7H", "6H", "2s2", "6M", "4s1", "1f", "7M", "0f", "6s1", "3f", "2s3", "5s1", "4s2", "1t1", "7s1", "0t1",
+    "6s2", "3t1", "2f", "5f", "4s3", "1t2", "7f", "6s3", "0F", "2t1", "3t2", "5t1", "2F", "4f", "1t3", "7t1",
+    "4t1", "6f", "3t3", "5t2", "4F", "1F", "7t2", "6t1", "3F", "5t3", "7t3", "6F", "5F", "7F",
+)
 
 
 def wrap(index, size):
@@ -224,6 +233,25 @@
     def stay_copy(p, q, h):
         return pltpu.make_async_copy(piece(0, q, h), land.at[p, 2 * q + h], land_sem.at[p, 2 * q + h])
 
+    def emit(i):
+        for p in range(2):
+            if i >= DEEP:
+                for needed, copy in root_copies(p, (i - DEEP) // 2, (i - DEEP) % 2):
+
+                    @pl.when(needed)
+                    def _(copy=copy):
+                        copy.wait_send()
+
+            for needed, copy in root_copies(p, i // 2, i % 2):
+
+                @pl.when(needed)
+                def _(copy=copy):
+                    copy.start()
+
+            @pl.when(both(is_root[p], here[p]))
+            def _(p=p):
+                stay_copy(p, i // 2, i % 2).start()
+
     for q in range(WAVES):
         fetches[q].wait()
 
@@ -238,17 +266,8 @@
         lax.fori_loop(0, NZ, decode, 0)
         if q == 0:
             pl.semaphore_wait(barrier, expected)
-        for p in range(2):
-            for h in range(2):
-                for needed, copy in root_copies(p, q, h):
-
-                    @pl.when(needed)
-                    def _(copy=copy):
-                        copy.start()
-
-                @pl.when(both(is_root[p], here[p]))
-                def _(p=p, q=q, h=h):
-                    stay_copy(p, q, h).start()
+            emit(0)
+            emit(1)
 
     def relay(q, h):
         for p in range(2):
@@ -259,23 +278,29 @@
                     pltpu.make_async_copy(hold.at[slot, q, h], hold.at[slot, q, h], hold_sem.at[slot, q, h]).wait()
                     copy.start()
 
+    busy = [both(x == 0, distance(p, z) == 0) for p in range(2)]
+
     def passes(p, i):
-        onward, last = (1, NY - 1) if p == 0 else (-1, 1)
-        for slot, (needed, peer) in enumerate(((dy[p] != last, along_y(onward)), (dy[p] >= 0, other))):
+        pull = i % 2
+        up = both(jnp.logical_not(busy[p]), jnp.logical_or(dy[p] == 0, both(dy[p] == 1, pull == 0)))
+        down = jnp.logical_or(dy[p] == 0, both(dy[p] == NY - 1, pull == 1))
+        down = jnp.where(busy[p], dy[p] != 1, down)
+        for slot, (needed, peer) in enumerate(((up, along_y(1)), (down, along_y(-1)), (dy[p] >= 0, other))):
             copy = give(land.at[p, i], land.at[p, i], pass_sem.at[p, i, slot], land_sem.at[p, i], peer)
             yield both(match, needed), copy
 
     def hops(p):
         even = jnp.where(distance(p, z) == 0, jnp.where(x == 0, 0, 2), jnp.where(moved(p, z), 2, 1))
         at_first = jnp.where(odd, jnp.where(distance(p, z) == 0, 1, 2), even)
-        return at_first + (dy[p] if p == 0 else wrap(-dy[p], NY)) + 1 - match.astype(jnp.int32)
+        return at_first + jnp.where(both(dy[p] == 1, jnp.logical_not(busy[p])), 1, wrap(-dy[p], NY)) + 1 - match.astype(jnp.int32)
 
     away = [hops(p) for p in range(2)]
 
     def arrive(p, tick):
-        i = tick - away[p]
-
-        @pl.when(both(i >= 0, i < 2 * WAVES))
+        late = tick - HOP * away[p]
+        i = late // PACE
+
+        @pl.when(both(both(late >= 0, late % PACE == 0), i < 2 * WAVES))
         def _():
             pltpu.make_async_copy(land.at[p, i], land.at[p, i], land_sem.at[p, i]).wait()
             for needed, copy in passes(p, i):
@@ -289,18 +314,18 @@
             block = land[p, 2 * q + k // 2, 2 * (k % 2) : 2 * (k % 2) + 2].reshape(LANES, 2 * LANES)
             real, imag = block[:, :LANES], block[:, LANES:]
             at = 2 * LANES * k
-            rhs[p, at : at + LANES, :] = block
-            rhs[p, at + LANES : at + 2 * LANES, :LANES] = -imag
-            rhs[p, at + LANES : at + 2 * LANES, LANES:] = real
-
-    def product(p, rows):
-        return jnp.dot(rows.reshape(8 * 64, 8 * LANES), rhs[p], preferred_element_type=jnp.float32)
+            rhs[q, p, at : at + LANES, :] = block
+            rhs[q, p, at + LANES : at + 2 * LANES, :LANES] = -imag
+            rhs[q, p, at + LANES : at + 2 * LANES, LANES:] = real
+
+    def product(w, p, rows):
+        return jnp.dot(rows.reshape(8 * 64, 8 * LANES), rhs[w, p], preferred_element_type=jnp.float32)
 
     def multiply_z(slot, start, count):
         def block(k, _):
             pair = [wrap(z + NZ // 2 + 2 * k + i, NZ) for i in range(2)]
             rows = jnp.concatenate([mine[zd] for zd in pair], axis=0)
-            terms = product(0, rows).reshape(2, 4, 64, 2 * LANES)
+            terms = product(slot, 0, rows).reshape(2, 4, 64, 2 * LANES)
             for i, zd in enumerate(pair):
                 part[slot, 0, zd] = terms[i]
             return _
@@ -310,7 +335,7 @@
     def multiply_x(slot, start, count):
         def block(k, _):
             xd = wrap(x + NX // 2 + k, NX)
-            part[slot, 1, :, xd] = product(1, mine[:, xd]).reshape(8, 64, 2 * LANES)
+            part[slot, 1, :, xd] = product(slot, 1, mine[:, xd]).reshape(8, 64, 2 * LANES)
             return _
 
         lax.fori_loop(start, start + count, block, 0)
@@ -353,52 +378,36 @@
 
         return put
 
-    def heads(w):
-        first_z, first_x, _, _ = all_chains[w]
-        build(0, w)
-        multiply_z(w, 0, 1)
-        first_z.step(0)
-        build(1, w)
-        multiply_x(w, 0, 1)
-        first_x.step(0)
-
-    def rest(w):
-        multiply_z(w, 1, 3)
-        multiply_x(w, 1, 3)
-
-    def run(w, k):
-        first_z, first_x, then_x, then_z = all_chains[w]
-        slot = w
-        if 1 <= k <= 3:
-            first_z.step(k)
-        if k == 1:
-            first_x.step(1)
-        if k == 2:
-            first_x.finish(keep(slot, 1))
-        if 2 <= k <= 5:
-            then_z.step(k - 2)
-        if k == 4:
-            first_z.finish(keep(slot, 0))
-        if 4 <= k <= 5:
-            then_x.step(k - 4)
-        if k == 6:
-            then_x.finish(result(0, w))
-            then_z.finish(result(1, w))
-
-    for tick in range(FAR + SPAN * (WAVES - 1) + 8):
-        if 1 <= tick <= 2 * WAVES:
-            relay((tick - 1) // 2, (tick - 1) % 2)
-        if tick < 2 * WAVES + FAR:
+    def run(group, op):
+        w, which = group // 2, group % 2
+        first, then = (all_chains[w][0], all_chains[w][2]) if which == 0 else (all_chains[w][1], all_chains[w][3])
+        multiply = multiply_x if which else multiply_z
+        if op == "H":
+            build(which, w)
+            multiply(w, 0, 1)
+            first.step(0)
+        elif op == "M":
+            multiply(w, 1, 3)
+        elif op == "f":
+            first.finish(keep(w, which))
+            then.step(0)
+        elif op == "F":
+            then.finish(result(which, w))
+        else:
+            (first if op[0] == "s" else then).step(int(op[1]))
+
+    for token in ORDER:
+        if token[0] == "k":
+            tick = int(token[1:])
+            if tick % PACE == 0 and 2 <= tick // PACE < 2 * WAVES:
+                emit(tick // PACE)
+            at = tick - HOP
+            if at >= 0 and at % PACE == 0 and at // PACE < 2 * WAVES:
+                relay(at // PACE // 2, at // PACE % 2)
             for p in range(2):
                 arrive(p, tick)
-        for w in range(WAVES):
-            k = tick - FAR - 1 - SPAN * w
-            if k == 0:
-                heads(w)
-            if 1 <= k <= 6:
-                run(w, k)
-            if k == 0:
-                rest(w)
+        else:
+            run(int(token[0]), token[1:])
 
     for group in all_chains:
         for chain in group:
@@ -406,7 +415,9 @@
     for p in range(2):
         for q in range(WAVES):
             for h in range(2):
-                sent = [*root_copies(p, q, h), *passes(p, 2 * q + h)]
+                sent = [*passes(p, 2 * q + h)]
+                if 2 * q + h >= 2 * WAVES - DEEP:
+                    sent += root_copies(p, q, h)
                 sent += [(needed, copy) for needed, _, copy in relay_copies(p, q, h)]
                 for needed, copy in sent:
 
@@ -434,7 +445,7 @@
             pltpu.VMEM((NZ, NX, 64, 1024), bf16),
             pltpu.VMEM((2, 2 * WAVES, NX, 64, n), bf16),
             pltpu.VMEM((2, WAVES, 2, NX, 64, n), bf16),
-            pltpu.VMEM((2, 1024, n), bf16),
+            pltpu.VMEM((WAVES, 2, 1024, n), bf16),
             pltpu.VMEM((WAVES, 2, NZ, NX, 64, n), f32),
             pltpu.VMEM((WAVES, 2, NZ, 2, 32, n), f32),
             pltpu.VMEM((WAVES, 2, NZ // 2, NX, 64, n), bf16),
@@ -450,7 +461,7 @@
             dma((2, 2 * WAVES)),
             dma((2, WAVES, 2)),
             dma((2, 2, WAVES, 2)),
-            dma((2, 2 * WAVES, 2)),
+            dma((2, 2 * WAVES, 3)),
             dma((WAVES, 2, NZ // 2)),
             dma((WAVES, 2, NZ // 2)),
             dma((WAVES, 2, NX // 2)),

time: 128 us -> 110 us (0.86)
  Pallas kernels: 125 us -> 105 us
    pallas_call x1, Pallas kernels: 125 us -> 105 us  [on_device(): pl.pallas_call(kernel, out_shape=jax.ShapeDtypeStruct((2, 2, 64, 512), bf...]
where the time goes in v3:
time: 110 us; the launch traced here: 108 us
  Pallas kernels  105 us (95%)
  local copies, waits for them, and re-layouts  2.98 us (3%)
    pallas_call x1, Pallas kernels, on_device(): pl.pallas_call(kernel, out_shape=jax.ShapeDtypeStruct((2, 2, 64, 512), bf...  105 us
    unnamed x2, local copies, waits for them, and re-layouts  2.98 us

profile of v3, /device:TPU:8, one launch (start us, length us, event | category | flops | bytes accessed | tf_op | source)
XLA Modules:
  0.0 108.4 jit_solution(12835423429066336472)
XLA Ops:
  0.0 1.3 %copy.4.exp_ref = s32[4,1]{1,0:T(4,128)} copy(s32[4,1]{0,1:T(1,128)} %param.5) | data formatting | bytes 32 | tf_op args[2]
  1.3 105.4 %shard_map.37 = bf16[2,2,64,512]{3,2,1,0:T(8,128)(2,1)} custom-call(bf16[2,8,4,64,512]{4,3,2,1,0:T(8,128)(2,1)} %bitcast.1, s32[4,512]{1,0:T(4,128)} %occ_ref.1, s32[4,1]{1,0:T(4,128)} %copy.4.exp_ref), custom_call_target="tpu_custom_call" | custom-call | tf_op jit(solution)/shard_map/pallas_call | solution.py:433
  106.8 1.7 %copy.6 = bf16[2,2,64,512]{3,2,1,0:T(8,128)(2,1)} copy(bf16[2,2,64,512]{3,2,1,0:T(8,128)(2,1)} %shard_map.37) | data formatting | bytes 524288

commit v4 on v3

v4 whole, which is shorter than its diff:
```python
import functools

import jax
import jax.numpy as jnp
from jax import lax
from jax.experimental import pallas as pl
from jax.experimental.pallas import tpu as pltpu
from jax.sharding import PartitionSpec as P

MESH = pl.DeviceIdType.MESH
NY, NZ, NX = 4, 8, 4
WAVES = 4
LANES = 128
PARTS = 4
ITEMS = PARTS * WAVES
PACE = 2
HOP = 5
DEEP = 4
EARLY = 99
KINDS = "ZXZXZXZX"
NUM_Z, NUM_X = KINDS.count("Z"), KINDS.count("X")
ORDER = (
    32, "0H", "0M", 34, "1H", "1M", 36, "0s1", 40, "2H", "1s1", 41, "2M", 42, "0s2", 43,
    "3H", "3M", 45, "2s1", 48, "4H", "4M", 50, "0s3", "1f", 51, "5H", "5M", 53, "2s2", "4s1",
    54, "3s1", 56, "7H", "6H", "0f", "5s1", "1t1", "6M", "7M", "2s3", "4s2", "3f", "6s1", "1t2", "7s1",
    "0t1", "2f", "4s3", "3t1", "5f", "6s2", "1t3", "4f", "7f", "3t2", "5t1", "0F", "2t1", "4t1", "6s3", "2F",
    "1F", "7t1", "3t3", "4F", "5t2", "6f", "7t2", "3F", "settle", "0drain", "1drain", "2drain", "3drain", "4drain", "5t3", "6t1",
    "7t3", "5F", "6F", "7F", "5drain", "6drain", "7drain",
)


def wrap(index, size):
    return lax.rem(index + size, size)


class Chain:
    def __init__(self, n, me, neighbour, own, groups, split, send, recv, send_sem, recv_sem):
        self.split = split
        self.n, self.me, self.neighbour, self.own, self.groups = n, me, neighbour, own, groups
        self.send, self.recv, self.send_sem, self.recv_sem = send, recv, send_sem, recv_sem
        self.started = []

    def half(self, side):
        size = self.groups // 2
        return pl.ds(size * side, size)

    def copy(self, side, step):
        if step == 0 or (self.split and step in (1, EARLY)):
            cut = self.half(1 - side if step == EARLY else side)
            at = min(step, 1)
            source, target = self.send.at[side, at, cut], self.recv.at[side, at, cut]
        else:
            source, target = self.send.at[side, step], self.recv.at[side, step]
        return pltpu.make_async_remote_copy(
            src_ref=source,
            dst_ref=target,
            send_sem=self.send_sem.at[side, min(step, self.n // 2)],
            recv_sem=self.recv_sem.at[side, min(step, self.n // 2)],
            device_id=self.neighbour(1 - 2 * side),
            device_id_type=MESH,
        )

    def landed(self, side, step):
        self.copy(side, step).wait_recv()
        if step == 1 and self.split:
            self.copy(side, EARLY).wait_recv()

    def step(self, step):
        for side in range(2):
            slot = min(step, 1) if step == EARLY else step
            away = self.n // 2 - slot
            dest = wrap(self.me + (1 - 2 * side) * away, self.n)
            size = self.groups // 2
            halves = (side, 1 - side) if step else (side,)
            if self.split and step == 1:
                halves = (side,)
            if step == EARLY:
                halves = (1 - side,)
            elif step:
                self.landed(side, step - 1)
            for part in halves:
                with_received = step != EARLY and (step > 1 or (step == 1 and part == side))

                def block(g, _, part=part, with_received=with_received, dest=dest, side=side, slot=slot):
                    at = part * size + g
                    value = self.own(dest, at)
                    if with_received:
                        value = value + self.recv[side, step - 1, at].astype(jnp.float32)
                    self.send[side, slot, at] = value.astype(jnp.bfloat16)
                    return _

                lax.fori_loop(0, size, block, 0)
            copy = self.copy(side, step)
            copy.start()
            self.started.append(copy)

    def finish(self, put):
        last = self.n // 2 - 1
        for side in range(2):
            self.landed(side, last)

        def block(g, _):
            value = self.own(self.me, g)
            for side in range(2):
                value = value + self.recv[side, last, g].astype(jnp.float32)
            put(g, value)
            return _

        lax.fori_loop(0, self.groups, block, 0)

    def drain(self):
        for copy in self.started:
            copy.wait_send()


def kernel(
    raw_ref, occ_ref, exp_ref, out_ref,
    power_of, power_sem, raw, factor, mine, land, hold, rhs, part, summed,
    z_send, z_recv, x_send, x_recv, zx_send, zx_recv, xz_send, xz_recv,
    raw_sem, root_sem, land_sem, hold_sem, relay_sem, pass_sem,
    z_ss, z_rs, x_ss, x_rs, zx_ss, zx_rs, xz_ss, xz_rs,
):
    row, col = lax.axis_index("row"), lax.axis_index("col")
    y, core, z, x = row // 2, row % 2, col // NX, col % NX

    def device(y, core, z, x):
        return (wrap(y, NY) * 2 + core, wrap(z, NZ) * NX + wrap(x, NX))

    def along_z(step):
        return device(y, core, z + step, x)

    def along_x(step):
        return device(y, core, z, x + step)

    def along_y(step):
        return device(y + step, core, z, x)

    other = device(y, 1 - core, z, x)
    fetches = [
        pltpu.make_async_copy(
            raw_ref.at[:, :, :, :, pl.ds(LANES * q, LANES)],
            raw.at[:, :, :, :, pl.ds(LANES * q, LANES)],
            raw_sem.at[q],
        )
        for q in range(WAVES)
    ]
    for fetch in fetches:
        fetch.start()

    barrier = pltpu.get_barrier_semaphore()
    for peer in (along_z(1), along_z(-1), along_x(1), along_x(-1), along_y(1), along_y(-1), other):
        pl.semaphore_signal(barrier, inc=1, device_id=peer, device_id_type=MESH)
    expected = jnp.int32(7)
    both = jnp.logical_and
    root_col = [p * (NZ * NX // 2) for p in range(2)]
    is_root = [col == c for c in root_col]
    odd = x % 2 == 1

    def distance(p, plane):
        return wrap(plane - p * (NZ // 2), NZ)

    def moved(p, plane):
        d = distance(p, plane)
        return jnp.logical_or(jnp.logical_or(d == 3, d == 4), d == 7)

    prior = wrap(row - 2, NZ)
    here = [distance(p, row) == 0 for p in range(2)]
    direct = [both(is_root[p], jnp.logical_not(moved(p, row))) for p in range(2)]
    relay_x = [
        both(jnp.logical_or(col == root_col[p] + 1, col == root_col[p] + 3), jnp.logical_not(here[p]))
        for p in range(2)
    ]
    relay_n = [both(col == root_col[p] + 3, here[p]) for p in range(2)]
    relay_y = [both(is_root[p], moved(p, prior)) for p in range(2)]
    match = core == z % 2
    dy = [wrap(y - z // 2 - both(jnp.logical_not(odd), moved(p, z)).astype(jnp.int32), NY) for p in range(2)]
    first = [both(match, dy[p] == 0) for p in range(2)]

    greet = []
    for p in range(2):
        greet.append((both(direct[p], jnp.logical_not(here[p])), row * NX))
        greet.append((direct[p], row * NX + 2))
        greet.append((relay_x[p], row * NX + x))
        greet.append((relay_y[p], prior * NX))
        greet.append((relay_y[p], prior * NX + 2))
        near = both(distance(p, z) == 0, x != 2)
        greet.append((both(first[p], jnp.logical_not(near)), root_col[p] + jnp.where(odd, x, 0)))
    for needed, peer in greet:
        expected = expected + needed.astype(jnp.int32)

        @pl.when(needed)
        def _(peer=peer):
            pl.semaphore_signal(barrier, inc=1, device_id=(row, peer), device_id_type=MESH)

    powers = pltpu.make_async_copy(exp_ref, power_of, power_sem)
    powers.start()
    powers.wait()
    present = occ_ref[...].astype(jnp.float32)
    for tile in range(NZ // 2):
        exponent = power_of[tile, 0]
        scale = jnp.float32(1.0)
        for power in (-2, -1, 1, 2):
            scale = jnp.where(exponent == power, jnp.float32(2.0**power), scale)
        factor[tile] = present[tile : tile + 1] * scale

    def piece(j, i):
        lanes = pl.ds(pl.multiple_of(2 * LANES * (i // PARTS), 2 * LANES), 2 * LANES)
        part_of = i % PARTS
        return mine.at[2 * j + part_of // 2, pl.ds(2 * (part_of % 2), 2), :, lanes]

    def give(source, target, send_sem, recv_sem, peer):
        return pltpu.make_async_remote_copy(
            src_ref=source, dst_ref=target, send_sem=send_sem, recv_sem=recv_sem,
            device_id=peer, device_id_type=MESH,
        )

    side = col // (NZ * NX // 2)
    is_source = col % (NZ * NX // 2) == 0
    at_home = distance(side, row) == 0
    shifted = moved(side, row)
    plain = both(jnp.logical_not(at_home), jnp.logical_not(shifted))
    carries_x = both(x % 2 == 1, both(z % (NZ // 2) == 0, jnp.logical_not(at_home)))
    carries_y = both(is_source, moved(side, prior))
    carries_n = both(x == 3, both(z % (NZ // 2) == 0, at_home))
    base_col = side * (NZ * NX // 2)

    def root_copies(i):
        def to(j, target, recv_sem, peer):
            return give(piece(j, i), target, root_sem.at[i, j], recv_sem, peer)

        held = hold.at[0, i], hold_sem.at[0, i]
        held_too = hold.at[1, i], hold_sem.at[1, i]
        landed = land.at[side, i], land_sem.at[side, i]
        for j in (1, 3):
            yield jnp.logical_not(at_home), to(j, *held, (row, base_col + j))
            yield at_home, to(j, *landed, (row, base_col + j))
        yield plain, to(0, *landed, (row, row * NX))
        yield plain, to(2, *landed, (row, row * NX + 2))
        yield shifted, to(0, *held, along_y(1))
        yield shifted, to(2, *held_too, along_y(1))
        yield both(at_home, i % 2 == 0), to(2, *landed, (row, row * NX + 2))
        yield both(at_home, i % 2 == 1), to(2, *held_too, (row, base_col + 3))

    def relay_copies(i):
        for needed, kind, slot, target in (
            (carries_x, 0, 0, row * NX + x),
            (carries_y, 1, 0, prior * NX),
            (carries_y, 1, 1, prior * NX + 2),
            (both(carries_n, i % 2 == 1), 0, 1, row * NX + 2),
        ):
            yield needed, slot, give(
                hold.at[slot, i], land.at[side, i], relay_sem.at[kind, slot, i], land_sem.at[side, i], (row, target)
            )

    def all_sent(copies):
        for needed, copy in copies:

            @pl.when(needed)
            def _(copy=copy):
                copy.wait_send()

    def emit(i):
        @pl.when(is_source)
        def _():
            @pl.when(i >= DEEP)
            def _():
                all_sent(root_copies(i - DEEP))

            for needed, copy in root_copies(i):

                @pl.when(needed)
                def _(copy=copy):
                    copy.start()

            @pl.when(at_home)
            def _():
                pltpu.make_async_copy(piece(0, i), land.at[side, i], land_sem.at[side, i]).start()

    for q in range(WAVES):
        fetches[q].wait()

        def decode(zd, _, q=q):
            f = factor[zd // 2, :, LANES * q : LANES * (q + 1)]
            for half in range(2):
                value = raw[half, zd, :, :, LANES * q : LANES * (q + 1)].astype(jnp.float32)
                start = 2 * LANES * q + LANES * half
                mine[zd, :, :, start : start + LANES] = (value * f[None]).astype(jnp.bfloat16)
            return _

        lax.fori_loop(0, NZ, decode, 0)
        if q == 0:
            pl.semaphore_wait(barrier, expected)
            for i in range(DEEP):
                emit(jnp.int32(i))

    carries = jnp.logical_or(carries_x, jnp.logical_or(carries_y, carries_n))

    def relay(i):
        @pl.when(carries)
        def _():
            for needed, slot, copy in relay_copies(i):

                @pl.when(needed)
                def _(copy=copy, slot=slot):
                    pltpu.make_async_copy(hold.at[slot, i], hold.at[slot, i], hold_sem.at[slot, i]).wait()
                    copy.start()

    busy = [both(x == 0, distance(p, z) == 0) for p in range(2)]

    def passes(p, i):
        pull = i % 2
        up = both(jnp.logical_not(busy[p]), jnp.logical_or(dy[p] == 0, both(dy[p] == 1, pull == 0)))
        down = jnp.logical_or(dy[p] == 0, both(dy[p] == NY - 1, pull == 1))
        down = jnp.where(busy[p], dy[p] != 1, down)
        for slot, (needed, peer) in enumerate(((up, along_y(1)), (down, along_y(-1)), (dy[p] >= 0, other))):
            copy = give(land.at[p, i], land.at[p, i], pass_sem.at[p, i, slot], land_sem.at[p, i], peer)
            yield needed, copy

    def hops(p):
        even = jnp.where(distance(p, z) == 0, jnp.where(x == 0, 0, 2), jnp.where(moved(p, z), 2, 1))
        at_first = jnp.where(odd, jnp.where(distance(p, z) == 0, 1, 2), even)
        return at_first + jnp.where(both(dy[p] == 1, jnp.logical_not(busy[p])), 1, wrap(-dy[p], NY)) + 1 - match.astype(jnp.int32)

    away = [hops(p) for p in range(2)]

    def arrive(p, tick):
        late = tick - HOP * away[p]
        i = late // PACE

        @pl.when(both(both(late >= 0, late % PACE == 0), i < ITEMS))
        def _():
            pltpu.make_async_copy(land.at[p, i], land.at[p, i], land_sem.at[p, i]).wait()

            @pl.when(match)
            def _():
                for needed, copy in passes(p, i):

                    @pl.when(needed)
                    def _(copy=copy):
                        copy.start()

    def build(p, q):
        for k in range(4):
            block = land[p, PARTS * q + k].reshape(LANES, 2 * LANES)
            real, imag = block[:, :LANES], block[:, LANES:]
            at = 2 * LANES * k
            rhs[q, p, at : at + LANES, :] = block
            rhs[q, p, at + LANES : at + 2 * LANES, :LANES] = -imag
            rhs[q, p, at + LANES : at + 2 * LANES, LANES:] = real

    def product(w, p, rows):
        return jnp.dot(rows.reshape(8 * 64, 8 * LANES), rhs[w, p], preferred_element_type=jnp.float32)

    def multiply_z(slot, which, start, count):
        def block(k, _):
            pair = [wrap(z + NZ // 2 + 2 * k + i, NZ) for i in range(2)]
            rows = jnp.concatenate([mine[zd] for zd in pair], axis=0)
            terms = product(slot, which, rows).reshape(2, 4, 64, 2 * LANES)
            for i, zd in enumerate(pair):
                part[slot, which, zd] = terms[i]
            return _

        lax.fori_loop(start, start + count, block, 0)

    def multiply_x(slot, which, start, count):
        def block(k, _):
            xd = wrap(x + NX // 2 + k, NX)
            part[slot, which, :, xd] = product(slot, which, mine[:, xd]).reshape(8, 64, 2 * LANES)
            return _

        lax.fori_loop(start, start + count, block, 0)

    def chains(group):
        w, which, kind, nth = group // 2, group % 2, KINDS[group], KINDS[:group].count(KINDS[group])
        if kind == "Z":
            first = Chain(
                NZ, z, along_z, lambda d, g: part[w, which, d, g], NX, True,
                z_send.at[nth], z_recv.at[nth], z_ss.at[nth], z_rs.at[nth],
            )
            then = Chain(
                NX, x, along_x, lambda d, g: summed[w, which, d, g], 2, False,
                zx_send.at[nth], zx_recv.at[nth], zx_ss.at[nth], zx_rs.at[nth],
            )
        else:
            first = Chain(
                NX, x, along_x, lambda d, g: part[w, which, g, d], NZ, True,
                x_send.at[nth], x_recv.at[nth], x_ss.at[nth], x_rs.at[nth],
            )
            then = Chain(
                NZ, z, along_z, lambda d, g: summed[w, which, d, g], 2, False,
                xz_send.at[nth], xz_recv.at[nth], xz_ss.at[nth], xz_rs.at[nth],
            )
        return first, then

    all_chains = [chains(group) for group in range(2 * WAVES)]

    def keep(slot, which):
        def put(g, value):
            summed[slot, which, g] = value.reshape(2, 32, 2 * LANES)

        return put

    def result(p, w):
        def put(g, value):
            value = value.astype(jnp.bfloat16)
            for half in range(2):
                out_ref[p, half, pl.ds(pl.multiple_of(32 * g, 32), 32), LANES * w : LANES * (w + 1)] = value[
                    :, LANES * half : LANES * (half + 1)
                ]

        return put

    def run(group, op):
        w, which = group // 2, group % 2
        first, then = all_chains[group]
        multiply = multiply_z if KINDS[group] == "Z" else multiply_x
        if op == "H":
            build(which, w)
            multiply(w, which, 0, 1)
            first.step(0)
        elif op == "M":
            multiply(w, which, 1, 3)
            first.step(EARLY)
        elif op == "f":
            first.finish(keep(w, which))
            then.step(0)
        elif op == "F":
            then.finish(result(which, w))
        else:
            (first if op[0] == "s" else then).step(int(op[1]))

    def spread(tick, carry):
        i = tick // PACE

        @pl.when(both(tick % PACE == 0, both(i >= DEEP, i < ITEMS)))
        def _():
            emit(i)

        held = (tick - HOP) // PACE

        @pl.when(both((tick - HOP) % PACE == 0, both(tick >= HOP, held < ITEMS)))
        def _():
            relay(held)

        for p in range(2):
            arrive(p, tick)
        return carry

    def settle(i, carry):
        @pl.when(match)
        def _():
            for p in range(2):
                all_sent(passes(p, i))

        @pl.when(carries)
        def _():
            all_sent((needed, copy) for needed, _, copy in relay_copies(i))

        @pl.when(both(is_source, i >= ITEMS - DEEP))
        def _():
            all_sent(root_copies(i))

        return carry

    tick = 0
    for token in ORDER:
        if isinstance(token, int):
            lax.fori_loop(tick, token, spread, 0)
            tick = token
        elif token == "settle":
            lax.fori_loop(0, ITEMS, settle, 0)
        elif token[1:] == "drain":
            for chain in all_chains[int(token[0])]:
                chain.drain()
        else:
            run(int(token[0]), token[1:])


def on_device(raw_blocks, occupancy, exponent):
    bf16, f32 = jnp.bfloat16, jnp.float32
    dma = pltpu.SemaphoreType.DMA
    n = 2 * LANES
    return pl.pallas_call(
        kernel,
        out_shape=jax.ShapeDtypeStruct((2, 2, 64, 512), bf16),
        in_specs=[
            pl.BlockSpec(memory_space=pl.ANY),
            pl.BlockSpec(memory_space=pltpu.VMEM),
            pl.BlockSpec(memory_space=pl.ANY),
        ],
        out_specs=pl.BlockSpec(memory_space=pltpu.VMEM),
        scratch_shapes=[
            pltpu.SMEM((4, 1), jnp.int32),
            dma,
            pltpu.VMEM((2, NZ, NX, 64, 512), bf16),
            pltpu.VMEM((4, 1, 512), f32),
            pltpu.VMEM((NZ, NX, 64, 1024), bf16),
            pltpu.VMEM((2, ITEMS, 2, 64, n), bf16),
            pltpu.VMEM((2, ITEMS, 2, 64, n), bf16),
            pltpu.VMEM((WAVES, 2, 1024, n), bf16),
            pltpu.VMEM((WAVES, 2, NZ, NX, 64, n), f32),
            pltpu.VMEM((WAVES, 2, NZ, 2, 32, n), f32),
            pltpu.VMEM((NUM_Z, 2, NZ // 2, NX, 64, n), bf16),
            pltpu.VMEM((NUM_Z, 2, NZ // 2, NX, 64, n), bf16),
            pltpu.VMEM((NUM_X, 2, NX // 2, NZ, 64, n), bf16),
            pltpu.VMEM((NUM_X, 2, NX // 2, NZ, 64, n), bf16),
            pltpu.VMEM((NUM_Z, 2, NX // 2, 2, 32, n), bf16),
            pltpu.VMEM((NUM_Z, 2, NX // 2, 2, 32, n), bf16),
            pltpu.VMEM((NUM_X, 2, NZ // 2, 2, 32, n), bf16),
            pltpu.VMEM((NUM_X, 2, NZ // 2, 2, 32, n), bf16),
            dma((WAVES,)),
            dma((ITEMS, NX)),
            dma((2, ITEMS)),
            dma((2, ITEMS)),
            dma((2, 2, ITEMS)),
            dma((2, ITEMS, 3)),
            dma((NUM_Z, 2, NZ // 2 + 1)),
            dma((NUM_Z, 2, NZ // 2 + 1)),
            dma((NUM_X, 2, NX // 2 + 1)),
            dma((NUM_X, 2, NX // 2 + 1)),
            dma((NUM_Z, 2, NX // 2)),
            dma((NUM_Z, 2, NX // 2)),
            dma((NUM_X, 2, NZ // 2)),
            dma((NUM_X, 2, NZ // 2)),
        ],
        compiler_params=pltpu.CompilerParams(
            collective_id=0, has_side_effects=True, vmem_limit_bytes=60 * 2**20
        ),
    )(raw_blocks.reshape(2, NZ, NX, 64, 512), occupancy, exponent)


def solution(mesh):
    placed = (P(None, "row", "col"), P("row", "col"), P("row", "col"))
    return jax.shard_map(
        on_device,
        mesh=mesh,
        in_specs=placed,
        out_specs=P(None, None, ("row", "col"), None),
        check_vma=False,
    )
```

time: 110 us -> 106 us (0.964)
  Pallas kernels: 105 us -> 101 us
    pallas_call x1, Pallas kernels: 105 us -> 101 us  [on_device(): pl.pallas_call(kernel, out_shape=jax.ShapeDtypeStruct((2, 2, 64, 512), bf...]
where the time goes in v4:
time: 106 us; the launch traced here: 104 us
  Pallas kernels  101 us (95%)
  local copies, waits for them, and re-layouts  2.98 us (3%)
    pallas_call x1, Pallas kernels, on_device(): pl.pallas_call(kernel, out_shape=jax.ShapeDtypeStruct((2, 2, 64, 512), bf...  101 us
    unnamed x2, local copies, waits for them, and re-layouts  2.98 us

profile of v4, /device:TPU:8, one launch (start us, length us, event | category | flops | bytes accessed | tf_op | source)
XLA Modules:
  0.0 104.0 jit_solution(17494549485278908508)
XLA Ops:
  0.0 1.3 %copy.4.exp_ref = s32[4,1]{1,0:T(4,128)} copy(s32[4,1]{0,1:T(1,128)} %param.5) | data formatting | bytes 32 | tf_op args[2]
  1.3 101.0 %shard_map.37 = bf16[2,2,64,512]{3,2,1,0:T(8,128)(2,1)} custom-call(bf16[2,8,4,64,512]{4,3,2,1,0:T(8,128)(2,1)} %bitcast.1, s32[4,512]{1,0:T(4,128)} %occ_ref.1, s32[4,1]{1,0:T(4,128)} %copy.4.exp_ref), custom_call_target="tpu_custom_call" | custom-call | tf_op jit(solution)/shard_map/pallas_call | solution.py:483
  102.3 1.7 %copy.6 = bf16[2,2,64,512]{3,2,1,0:T(8,128)(2,1)} copy(bf16[2,2,64,512]{3,2,1,0:T(8,128)(2,1)} %shard_map.37) | data formatting | bytes 524288

commit v5 on v4

--- a/solution.py
+++ b/solution.py
@@ -15,7 +15,7 @@
 ITEMS = PARTS * WAVES
 PACE = 2
 HOP = 5
-DEEP = 4
+DEEP = 8
 EARLY = 99
 KINDS = "ZXZXZXZX"
 NUM_Z, NUM_X = KINDS.count("Z"), KINDS.count("X")
@@ -290,8 +290,8 @@
         lax.fori_loop(0, NZ, decode, 0)
         if q == 0:
             pl.semaphore_wait(barrier, expected)
-            for i in range(DEEP):
-                emit(jnp.int32(i))
+        for i in range(PARTS * q, min(PARTS * (q + 1), DEEP)):
+            emit(jnp.int32(i))
 
     carries = jnp.logical_or(carries_x, jnp.logical_or(carries_y, carries_n))
 

time: 106 us -> 105 us (level); the launches traced: 104 us -> 104 us
  no operation moved by 1% of the time
where the time goes in v5:
time: 105 us; the launch traced here: 104 us
  Pallas kernels  101 us (96%)
  local copies, waits for them, and re-layouts  2.98 us (3%)
    pallas_call x1, Pallas kernels, on_device(): pl.pallas_call(kernel, out_shape=jax.ShapeDtypeStruct((2, 2, 64, 512), bf...  101 us
    unnamed x2, local copies, waits for them, and re-layouts  2.98 us

profile of v5, /device:TPU:8, one launch (start us, length us, event | category | flops | bytes accessed | tf_op | source)
XLA Modules:
  0.0 104.2 jit_solution(1964894821414451888)
XLA Ops:
  0.0 1.3 %copy.4.exp_ref = s32[4,1]{1,0:T(4,128)} copy(s32[4,1]{0,1:T(1,128)} %param.5) | data formatting | bytes 32 | tf_op args[2]
  1.3 101.3 %shard_map.37 = bf16[2,2,64,512]{3,2,1,0:T(8,128)(2,1)} custom-call(bf16[2,8,4,64,512]{4,3,2,1,0:T(8,128)(2,1)} %bitcast.1, s32[4,512]{1,0:T(4,128)} %occ_ref.1, s32[4,1]{1,0:T(4,128)} %copy.4.exp_ref), custom_call_target="tpu_custom_call" | custom-call | tf_op jit(solution)/shard_map/pallas_call | solution.py:483
  102.6 1.7 %copy.6 = bf16[2,2,64,512]{3,2,1,0:T(8,128)(2,1)} copy(bf16[2,2,64,512]{3,2,1,0:T(8,128)(2,1)} %shard_map.37) | data formatting | bytes 524288
